TPU v7x, 32 devices: a whole 2x2x4 slice. The times are simulated.
32 devices in a mesh: gx: 8 (over z, x), gy: 2 (over core), gz: 2 (over y).
Axes of the slice: x: 2, y: 2, z: 4, core: 2. Of those that a mesh axis runs over, the one named last changes fastest.
Arguments:
- features: bfloat16 [8, 2, 2, 128, 512], P('gx', 'gy', 'gz'), may hold values from -6 to 6
- fraction: bfloat16 [8, 2, 2, 3, 128], P('gx', 'gy', 'gz'), may hold values from 0 to 0.98828125
- cell_index: int32 [8, 2, 2, 3, 128], P('gx', 'gy', 'gz'), may hold values from 0 to 127, as said below
- species: int32 [8, 2, 2, 128], P('gx', 'gy', 'gz'), may hold values from 0 to 1
- octant_rows: int32 [8, 2, 2, 8, 14], P('gx', 'gy', 'gz'), may hold values from 0 to 127, as said below
- neighbours: int32 [8, 2, 2, 16, 128], P('gx', 'gy', 'gz'), may hold values from 0 to 912, as said below
- radial_in: bfloat16 [2, 8, 64], replicated, may hold values from -2 to 2
- radial_out: bfloat16 [2, 64, 512], replicated, may hold values from -1.5 to 1.5
- mix_weight: bfloat16 [2, 2, 128, 128], replicated, may hold values from -0.5 to 0.5
- readout: bfloat16 [128, 2], replicated, may hold values from -0.125 to 0.125
- species_table: float32 [2, 2], replicated, may hold values from -4 to 4
Outputs:
- new_features: bfloat16 [8, 2, 2, 128, 512], P('gx', 'gy', 'gz')
- site_energy: float32 [8, 2, 2, 128], P('gx', 'gy', 'gz')
- recip_force: float32 [8, 2, 2, 3, 128], P('gx', 'gy', 'gz')
Inputs may be any that keep to these rules, and one draw needn't show every extreme that they name: `cell_index`: component x lies below 32, component y below 128, component z below 128. `octant_rows`: each octant's list holds 14 different atoms of the domain. `neighbours`: entries are rows of the domain's table; 912 is an empty slot; an atom never lists itself, and the other entries of a column are different; the cell of a listed row (cell_index plus its shift) lies within 8 cells of the atom's cell.
All inputs are finite; a program needn't handle non-finite values.
Results may differ from a plain program's by a relative error of at most 0.0051.
Values may be sent and summed in bfloat16 or wider, within the bound.
A program may use at most 128 MiB of HBM per device.

v0:
```python
import math

import jax
import jax.numpy as jnp
import numpy as np
from jax import lax
from jax.sharding import PartitionSpec as P

C = 128
NB = 8
LAYERS = 2
NEIGH = 16
ENV = 7
MESH = 256


COULOMB = 4.0
EWALD = 0.7
HIGHEST_PRECISION = lax.Precision.HIGHEST


def extended_2(shard, sides, width):
    for axis, dim in sides:
        count, length = (lax.axis_size(axis), shard.shape[dim])
        up = [(i, (i + 1) % count) for i in range(count)]
        down = [(j, i) for i, j in up]
        last = lax.slice_in_dim(shard, length - width, length, axis=dim)
        leading = lax.slice_in_dim(shard, 0, width, axis=dim)
        before = lax.ppermute(last, axis, up)
        after = lax.ppermute(leading, axis, down)
        shard = jnp.concatenate([before, shard, after], axis=dim)
    return shard


def from_partner(block, axis, bit):
    count = lax.axis_size(axis)
    route = []
    for low in range(count):
        high = low | 1 << bit
        if high != low and high < count:
            route += [(low, high), (high, low)]
    return lax.ppermute(block, axis, route)


def outer_cells():
    found = []
    for first in range(4):
        for second in range(4):
            for third in range(4):
                if 0 < first < 3 and 0 < second < 3 and (0 < third < 3):
                    continue
                found.append((first, second, third))
    return found


def offset_of(coord):
    return -1 if coord == 0 else 1 if coord == 3 else 0


def spline(fraction_in):
    lower_t = 1.0 - fraction_in
    weights = jnp.stack(
        [
            lower_t * lower_t * lower_t / 6.0,
            (3.0 * fraction_in * fraction_in * fraction_in - 6.0 * fraction_in * fraction_in + 4.0)
            / 6.0,
            (
                -3.0 * fraction_in * fraction_in * fraction_in
                + 3.0 * fraction_in * fraction_in
                + 3.0 * fraction_in
                + 1.0
            )
            / 6.0,
            fraction_in * fraction_in * fraction_in / 6.0,
        ]
    )
    slopes = jnp.stack(
        [
            -0.5 * lower_t * lower_t,
            0.5 * (3.0 * fraction_in * fraction_in - 4.0 * fraction_in),
            0.5 * (-3.0 * fraction_in * fraction_in + 2.0 * fraction_in + 1.0),
            0.5 * fraction_in * fraction_in,
        ]
    )
    return (weights, slopes)


def frequency(waves):
    signed = jnp.where(waves <= MESH // 2, waves, waves - MESH).astype(jnp.float32) / MESH
    modulus = 9.0 / jnp.square(2.0 + jnp.cos(waves.astype(jnp.float32) * (2.0 * math.pi / MESH)))
    return (signed, modulus)


def influence(wave_y, wave_z, wave_x):
    freq_y, modul_y = frequency(wave_y)
    freq_z, modul_z = frequency(wave_z)
    freq_x, modul_x = frequency(wave_x)
    wave_square = (
        jnp.square(freq_x)[None, None, :]
        + jnp.square(freq_y)[:, None, None]
        + jnp.square(freq_z)[None, :, None]
    )
    positive = wave_square > 0.0
    gaussian = jnp.exp(-(math.pi * math.pi / (EWALD * EWALD)) * wave_square)
    kernel = jnp.where(positive, gaussian / jnp.where(positive, wave_square, 1.0), 0.0)
    moduli = modul_x[None, None, :] * modul_y[:, None, None] * modul_z[None, :, None]
    return kernel * moduli * (COULOMB / (math.pi * MESH**3))


def interact(current, lookup, places, located, links, radial_in, radial_out, mix_weight):
    atom_count = current.shape[0]
    gathered = lookup[links].astype(jnp.float32)
    displace = places[links] - located[None]
    length_sq = jnp.sum(displace * displace, axis=-1)
    distance = jnp.sqrt(length_sq)
    direction = displace / jnp.sqrt(length_sq + 1.0)[..., None]
    spacing = ENV / (NB - 1)
    centres = jnp.arange(NB, dtype=jnp.float32) * spacing
    envelope = jnp.square(jnp.maximum(1.0 - length_sq / (ENV * ENV), 0.0))
    basis_set = (
        jnp.exp(-jnp.square((distance[..., None] - centres) / spacing)) * envelope[..., None]
    )
    edge_count = NEIGH * atom_count
    hidden = jax.nn.silu(
        jnp.dot(
            basis_set.reshape(edge_count, NB).astype(jnp.bfloat16),
            radial_in,
            preferred_element_type=jnp.float32,
        )
    ).astype(jnp.bfloat16)
    radial = jnp.dot(hidden, radial_out, preferred_element_type=jnp.float32).reshape(
        NEIGH, atom_count, 4 * C
    )
    scalars = gathered[..., :C]
    vectors = gathered[..., C:].reshape(NEIGH, atom_count, 3, C)
    first_path = radial[..., :C]
    second_path = radial[..., C : 2 * C]
    third_path = radial[..., 2 * C : 3 * C]
    fourth_path = radial[..., 3 * C :]
    projected = jnp.sum(direction[..., None] * vectors, axis=2)
    inverse_root = 1.0 / math.sqrt(NEIGH)
    scalar_message = jnp.sum(first_path * scalars + second_path * projected, axis=0) * inverse_root
    scaled_path = third_path * scalars
    vector_message = (
        jnp.einsum("kad,kac->adc", direction, scaled_path, precision=HIGHEST_PRECISION)
        + jnp.sum(fourth_path[:, :, None, :] * vectors, axis=0)
    ) * inverse_root
    previous = current.astype(jnp.float32)
    scalar_new = previous[:, :C] + jax.nn.silu(
        jnp.dot(
            scalar_message.astype(jnp.bfloat16), mix_weight[0], preferred_element_type=jnp.float32
        )
    )
    vector_new = previous[:, C:] + jnp.dot(
        vector_message.reshape(atom_count * 3, C).astype(jnp.bfloat16),
        mix_weight[1],
        preferred_element_type=jnp.float32,
    ).reshape(atom_count, 3 * C)
    return jnp.concatenate([scalar_new, vector_new], axis=1).astype(jnp.bfloat16)


def ghost_rows(buffer):
    return extended_2(buffer, (("gx", 0), ("gy", 1), ("gz", 2)), 1)


def mesh_rim(mesh_block):
    return extended_2(mesh_block, (("gx", 1), ("gy", 0), ("gz", 2)), 2)


def along_gy(term, row_count):
    return lax.psum_scatter(
        term(jnp.int32(0), lax.axis_size("gy") * row_count), "gy", scatter_dimension=0, tiled=True
    )


def across_gz(blocks):
    return lax.all_to_all(blocks, "gz", split_axis=0, concat_axis=0, tiled=True)


def across_gx(blocks):
    return lax.all_to_all(blocks, "gx", split_axis=0, concat_axis=0, tiled=True)


def outer_pick(extended):
    flattened = extended.reshape(64, -1)
    chosen = np.array(
        [16 * corner[0] + 4 * corner[1] + corner[2] for corner in outer_cells()], np.int32
    )
    return flattened[chosen]


def fold_rim(bordered, axis_dim):
    inner = bordered.shape[axis_dim] - 8
    middle = lax.slice_in_dim(bordered, 4, inner + 4, axis=axis_dim)
    lower = lax.slice_in_dim(bordered, 0, 2, axis=axis_dim)
    higher = lax.slice_in_dim(bordered, inner + 6, inner + 8, axis=axis_dim)
    shape_pad = list(lower.shape)
    shape_pad[axis_dim] = inner - 2
    padding = jnp.zeros(shape_pad, bordered.dtype)
    return (
        middle
        + jnp.concatenate([lower, padding], axis=axis_dim)
        + jnp.concatenate([padding, higher], axis=axis_dim)
    )


def product(left, right):
    return jnp.dot(left, right, precision=HIGHEST_PRECISION, preferred_element_type=jnp.float32)


def phases(left, right):
    turns = left[:, None] * right[None, :] % MESH
    angle = turns.astype(jnp.float32) * (2.0 * math.pi / MESH)
    return (jnp.cos(angle), jnp.sin(angle))


def along_last(data, cosine_table, sine_table, inverse):
    flattened = data.reshape(-1, data.shape[-1])
    with_cosine = product(flattened, cosine_table).reshape(data.shape)
    with_sine = product(flattened, sine_table).reshape(data.shape)
    if inverse:
        real_part = with_cosine[:, 0] - with_sine[:, 1]
        imag_part = with_cosine[:, 1] + with_sine[:, 0]
    else:
        real_part = with_cosine[:, 0] + with_sine[:, 1]
        imag_part = with_cosine[:, 1] - with_sine[:, 0]
    return jnp.stack([real_part, imag_part], axis=1)


def spline_rows(coefficient, cell_row, span):
    slot_index = jnp.arange(span + 4, dtype=jnp.int32)
    summed = jnp.zeros((cell_row.shape[0], span + 4), jnp.float32)
    for offset in range(4):
        summed = summed + coefficient[offset][:, None] * (
            slot_index[None, :] == (cell_row + 1 + offset)[:, None]
        ).astype(jnp.float32)
    return summed


def per_device(
    features,
    fraction,
    cell_index,
    species,
    octant_rows,
    neighbours,
    radial_in,
    radial_out,
    mix_weight,
    readout,
    species_table,
):
    current = features[0, 0, 0]
    fraction_here = fraction[0, 0, 0]
    cells_here = cell_index[0, 0, 0]
    kinds = species[0, 0, 0]
    chosen_rows = octant_rows[0, 0, 0].reshape(-1)
    links = neighbours[0, 0, 0]
    atom_count, feat_width = current.shape
    ghost_count = chosen_rows.shape[0] // 8
    count_x = lax.axis_size("gx")
    count_y = lax.axis_size("gy")
    count_z = lax.axis_size("gz")
    span_x = MESH // count_x
    span_y = MESH // count_y
    span_z = MESH // count_z
    located = jnp.transpose(cells_here.astype(jnp.float32)) + jnp.transpose(
        fraction_here.astype(jnp.float32)
    )
    geometry = jnp.concatenate([fraction_here, cells_here.astype(jnp.bfloat16)], axis=0)[
        :, chosen_rows
    ]
    geometry = jnp.transpose(geometry.reshape(6, 8, ghost_count), (1, 0, 2)).reshape(
        8, 6 * ghost_count
    )
    outgoing = current[chosen_rows].reshape(8, ghost_count * feat_width)
    arrived = outer_pick(
        ghost_rows(jnp.concatenate([outgoing, geometry], axis=1).reshape(2, 2, 2, -1))
    )
    split_at = ghost_count * feat_width
    ghost_feats = arrived[:, :split_at].reshape(56 * ghost_count, feat_width)
    ghost_geometry = arrived[:, split_at:].reshape(56, 6, ghost_count).astype(jnp.float32)
    shift_table = np.array(
        [[offset_of(coord) for coord in corner] for corner in outer_cells()], np.float32
    )
    shifts = jnp.asarray(shift_table) * jnp.array([span_x, span_y, span_z], jnp.float32)
    ghost_places = ghost_geometry[:, 3:6] + shifts[:, :, None] + ghost_geometry[:, 0:3]
    places = jnp.concatenate(
        [
            located,
            jnp.transpose(ghost_places, (0, 2, 1)).reshape(-1, 3),
            jnp.zeros((1, 3), jnp.float32),
        ],
        axis=0,
    )
    block_rows = min(64, atom_count)
    block_count = atom_count // block_rows
    for layer_index in range(LAYERS):
        if layer_index > 0:
            outgoing = current[chosen_rows].reshape(2, 2, 2, ghost_count * feat_width)
            ghost_feats = outer_pick(ghost_rows(outgoing)).reshape(56 * ghost_count, feat_width)
        lookup = jnp.concatenate(
            [current, ghost_feats, jnp.zeros((1, feat_width), jnp.bfloat16)], axis=0
        )

        def one_block(block_index, lookup=lookup, layer_index=layer_index, current=current):
            start = block_index * block_rows
            return interact(
                lax.dynamic_slice_in_dim(current, start, block_rows, 0),
                lookup,
                places,
                lax.dynamic_slice_in_dim(located, start, block_rows, 0),
                lax.dynamic_slice_in_dim(links, start, block_rows, 1),
                radial_in[layer_index],
                radial_out[layer_index],
                mix_weight[layer_index],
            )

        current = lax.map(one_block, jnp.arange(block_count, dtype=jnp.int32)).reshape(
            atom_count, feat_width
        )
    head_out = jnp.dot(current[:, :C], readout, preferred_element_type=jnp.float32)
    one_hot = (
        kinds[:, None] == jnp.arange(species_table.shape[0], dtype=jnp.int32)[None, :]
    ).astype(jnp.float32)
    species_term = jnp.dot(
        one_hot, species_table, precision=HIGHEST_PRECISION, preferred_element_type=jnp.float32
    )
    base_energy = head_out[:, 0] + species_term[:, 0]
    charge = head_out[:, 1] + species_term[:, 1]
    weights, slopes = spline(fraction_here.astype(jnp.float32))
    weight_x = spline_rows(weights[:, 0], cells_here[0], span_x)
    weight_y = spline_rows(weights[:, 1], cells_here[1], span_y)
    weight_z = spline_rows(weights[:, 2], cells_here[2], span_z)
    plane_xz = (weight_x[:, :, None] * weight_z[:, None, :]).reshape(atom_count, -1)
    spread = product(jnp.transpose(weight_y * charge[:, None]), plane_xz).reshape(
        span_y + 4, span_x + 4, span_z + 4
    )
    charge_mesh = fold_rim(fold_rim(fold_rim(mesh_rim(spread), 0), 1), 2)
    index_x = lax.axis_index("gx")
    index_y = lax.axis_index("gy")
    index_z = lax.axis_index("gz")
    flattened = charge_mesh.reshape(span_y, span_x * span_z)
    own_rows = index_y * span_y + jnp.arange(span_y, dtype=jnp.int32)
    partner = from_partner(flattened, "gy", 0)
    partner_rows = (1 - index_y) * span_y + jnp.arange(span_y, dtype=jnp.int32)
    cosine_own, sine_own = phases(own_rows, own_rows)
    cosine_other, sine_other = phases(own_rows, partner_rows)
    real_part = product(cosine_own, flattened) + product(cosine_other, partner)
    imag_part = -(product(sine_own, flattened) + product(sine_other, partner))
    spectrum = jnp.stack([real_part, imag_part], axis=1)
    wave_rows = span_y // count_z
    full_waves = jnp.arange(MESH, dtype=jnp.int32)
    cosine_full, sine_full = phases(full_waves, full_waves)
    received = across_gz(spectrum.reshape(count_z, wave_rows, 2, span_x, span_z))
    lines_z = jnp.transpose(received, (1, 2, 3, 0, 4)).reshape(wave_rows, 2, span_x, MESH)
    lines_z = along_last(lines_z, cosine_full, sine_full, False)
    sending = jnp.transpose(lines_z.reshape(wave_rows, 2, span_x, count_x, span_x), (3, 0, 1, 2, 4))
    received = across_gx(sending)
    lines_x = jnp.transpose(received, (1, 2, 4, 0, 3)).reshape(wave_rows, 2, span_x, MESH)
    lines_x = along_last(lines_x, cosine_full, sine_full, False)
    wave_y = index_y * span_y + index_z * wave_rows + jnp.arange(wave_rows, dtype=jnp.int32)
    wave_z = index_x * span_x + jnp.arange(span_x, dtype=jnp.int32)
    kernel = influence(wave_y, wave_z, full_waves)
    scaled = lines_x * kernel[:, None]
    lines_x = along_last(scaled, cosine_full, sine_full, True)
    sending = jnp.transpose(lines_x.reshape(wave_rows, 2, span_x, count_x, span_x), (3, 0, 1, 2, 4))
    received = across_gx(sending)
    lines_z = jnp.transpose(received, (1, 2, 4, 0, 3)).reshape(wave_rows, 2, span_x, MESH)
    lines_z = along_last(lines_z, cosine_full, sine_full, True)
    sending = jnp.transpose(lines_z.reshape(wave_rows, 2, span_x, count_z, span_z), (3, 0, 1, 2, 4))
    returned = across_gz(sending).reshape(span_y, 2, span_x * span_z)

    def backward_rows(start, row_count):
        spots = jnp.arange(row_count, dtype=jnp.int32)
        cosine_table, sine_table = phases(spots, own_rows)
        return product(cosine_table, returned[:, 0]) - product(sine_table, returned[:, 1])

    potential = along_gy(backward_rows, span_y).reshape(span_y, span_x, span_z)
    bordered = mesh_rim(potential).reshape(span_y + 4, -1)
    slope_x = spline_rows(slopes[:, 0], cells_here[0], span_x)
    slope_y = spline_rows(slopes[:, 1], cells_here[1], span_y)
    slope_z = spline_rows(slopes[:, 2], cells_here[2], span_z)
    level_y = product(weight_y, bordered)
    level_slope = product(slope_y, bordered)
    potential_at = jnp.sum(level_y * plane_xz, axis=1)
    field_x = -jnp.sum(
        level_y * (slope_x[:, :, None] * weight_z[:, None, :]).reshape(atom_count, -1), axis=1
    )
    field_y = -jnp.sum(level_slope * plane_xz, axis=1)
    field_z = -jnp.sum(
        level_y * (weight_x[:, :, None] * slope_z[:, None, :]).reshape(atom_count, -1), axis=1
    )
    recip_force = charge[None, :] * jnp.stack([field_x, field_y, field_z])
    site_energy = base_energy + 0.5 * charge * potential_at
    return (current[None, None, None], site_energy[None, None, None], recip_force[None, None, None])


def solution(mesh):
    in_specs = (
        P("gx", "gy", "gz", None, None),
        P("gx", "gy", "gz", None, None),
        P("gx", "gy", "gz", None, None),
        P("gx", "gy", "gz", None),
        P("gx", "gy", "gz", None, None),
        P("gx", "gy", "gz", None, None),
        P(),
        P(),
        P(),
        P(),
        P(),
    )
    out_specs = (
        P("gx", "gy", "gz", None, None),
        P("gx", "gy", "gz", None),
        P("gx", "gy", "gz", None, None),
    )
    return jax.shard_map(
        per_device, mesh=mesh, in_specs=in_specs, out_specs=out_specs, check_vma=False
    )
```

profile of v0, /device:TPU:0, one launch (start us, length us, event | category | flops | bytes accessed | tf_op | source)
XLA Modules:
  0.0 1015.7 jit_solution(13685656532844758736)
XLA Ops:
  12.6 6.0 collective-permute-start.1
  32.3 10.0 collective-permute-done.5
  42.3 9.4 collective-permute-done.4
  60.3 106.1 %while.20 = (s32[]{:T(128)}, bf16[2,64,512]{2,1,0:T(8,128)(2,1)}, s32[2]{0:T(128)}, bf16[128,512]{1,0:T(8,128)(2,1)}, s32[16,128]{1,0:T(8,128)S(1)}, /*index=5*/...) while((s32[]{:T(128)}, bf16[2,64,512]{2,1,0:T(8,128)(2,1)}, ...), condition=%wide.region_5.6_spmd, body=%wide.region_0.5_spmd.sunk | while | flops 84597768 | bytes 33572176 | solution.py:319
  62.3 5.1 gather_fusion
  115.4 5.1 gather_fusion
  169.4 5.2 collective-permute-start.7
  194.0 9.3 collective-permute-done.10
  212.7 106.7 %while.21 = (s32[]{:T(128)}, bf16[2,64,512]{2,1,0:T(8,128)(2,1)}, s32[2]{0:T(128)S(1)}, bf16[128,512]{1,0:T(8,128)(2,1)}, s32[16,128]{1,0:T(8,128)S(1)}, /*index...) while((s32[]{:T(128)}, bf16[2,64,512]{2,1,0:T(8,128)(2,1)}, ...), condition=%wide.region_11.12_spmd, body=%wide.region_6.11_spmd.sunk | while | flops 84597768 | bytes 33564072 | solution.py:319
  214.1 5.1 gather_fusion.2
  267.4 5.1 gather_fusion.2
  321.1 6.0 fusion.123
  327.1 5.1 collective-permute-start.13
  332.2 5.6 collective-permute-done.13
  337.8 4.9 collective-permute-done.12
  362.6 8.3 pad_maximum_fusion.1
  370.9 5.1 fusion.56
  400.1 51.3 %all_to_all.20 = f32[2,64,2,32,128]{4,3,1,2,0:T(8,128)S(1)} all-to-all(f32[2,64,2,32,128]{4,3,1,2,0:T(8,128)S(1)} %pad_maximum_fusion.3), channel_id=1, replica_groups=mesh['gx'=8,'gy'=2,'gz'=2] {'gz'}, dimensions={0} | all-to-all | bytes 8388608 | tf_op jit(solution)/shard_map/all_to_all | solution.py:177
  451.4 6.1 copy.217
  457.5 6.5 dot_general.110
  464.0 8.4 fusion.100
  485.9 6.3 copy_bitcast_fusion.2
  492.2 9.8 reshape.1559
  502.0 4.9 all-to-all-start.1
  508.2 91.9 %all-to-all-done.1 = f32[8,1,131072]{2,1,0:T(1,128)} async-done(((f32[8,1,131072]{2,1,0:T(1,128)}), f32[8,1,131072]{2,1,0:T(1,128)}, u32[]{:S(2)}, u32[]{:S(2)}) %all-to-all-start.1) | async-done | bytes 4194336 | tf_op jit(solution)/shard_map/all_to_all | solution.py:181
  600.6 14.2 %reduce.2 = f32[8,131072]{1,0:T(8,128)} reduce(f32[8,1,131072]{2,1,0:T(1,128)} %all-to-all-done.1, f32[]{:T(128)} %broadcast.1281), dimensions={1}, to_apply=%all_to_all.13.reduce_sub_computation | reduce | bytes 8388612 | tf_op jit(solution)/shard_map/all_to_all | solution.py:181
  614.8 8.8 reshape.1560
  628.1 8.2 copy.221
  636.3 7.3 copy.222
  643.6 8.4 fusion.98
  662.6 5.0 fusion.71
  676.5 6.3 copy_bitcast_fusion.1
  682.8 9.8 reshape.1561
  692.6 97.3 %all_to_all.21 = f32[8,1,131072]{2,1,0:T(1,128)} all-to-all(f32[8,1,131072]{2,1,0:T(1,128)} %reshape.1561), channel_id=1, replica_groups=mesh['gx'=8,'gy'=2,'gz'=2] {'gx'}, dimensions={0} | all-to-all | bytes 8388608 | tf_op jit(solution)/shard_map/all_to_all | solution.py:181
  790.0 13.8 %reduce.3 = f32[8,131072]{1,0:T(8,128)} reduce(f32[8,1,131072]{2,1,0:T(1,128)} %all_to_all.21, f32[]{:T(128)} %broadcast.1281), dimensions={1}, to_apply=%all_to_all.14.reduce_sub_computation | reduce | bytes 8388612 | tf_op jit(solution)/shard_map/all_to_all | solution.py:181
  803.8 8.8 reshape.1562
  817.0 8.2 copy.227
  825.3 7.3 copy.228
  832.6 8.3 fusion.95
  856.9 49.4 %all_to_all.22 = f32[2,64,2,32,128]{4,3,1,2,0:T(8,128)S(1)} all-to-all(f32[2,64,2,32,128]{4,3,1,2,0:T(8,128)S(1)} %maximum_bitcast_fusion.2), channel_id=1, replica_groups=mesh['gx'=8,'gy'=2,'gz'=2] {'gz'}, dimensions={0} | all-to-all | bytes 8388608 | tf_op jit(solution)/shard_map/all_to_all | solution.py:177
  908.7 5.0 reshape.1465
  913.7 5.8 fusion.77
  919.5 6.1 convolution_subtract_fusion
  925.6 10.9 %reduce-scatter.2.cloned.1.call-done = f32[128,4096]{1,0:T(8,128)} async-done(((f32[256,4096]{1,0:T(8,128)}), f32[128,4096]{1,0:T(8,128)}) %reduce-scatter.2.cloned.1.call-update) | async-done | bytes 2097168 | tf_op jit(solution)/shard_map/reduce_scatter | solution.py:171
  972.7 4.9 pad_maximum_fusion.2
  981.6 6.0 reshape.1467
  987.7 11.4 %multiply_reduce_fusion.7 = (f32[128]{0:T(128)S(1)}, f32[128]{0:T(128)S(1)}, f32[128]{0:T(128)S(1)}) fusion(f32[128,4752]{0,1:T(8,128)} %mul.1080, f32[128,4752]{0,1:T(8,128)} %mul.1109, f32[128,4752]{0,1:T(8,128)S(1)} %copy-done.6, f32[132,4752]{1,0:T(8,128)} %reshape.1467, f32[128]{0:T(128)S(1)} %copy-done.30, s32[128]{0:T(128)S(1)} %copy-done.27, ...), kind=kOutput, calls=%fused_computation.137 | convolution fusion | flops 967312512 | bytes 9813760 | tf_op jit(solution)/shard_map/dot_general | solution.py:208
  999.7 8.3 fusion.84
  (480 shorter events, 397.3 us)
Async XLA Ops:
  7.2 182.5 %copy-start = (f32[2,2]{1,0:T(2,128)S(1)}, f32[2,2]{1,0:T(2,128)}, u32[]{:S(2)}) copy-start(f32[2,2]{1,0:T(2,128)} %param.31) | copy-start | bytes 52
  7.2 19.5 %copy-start.22 = (s32[1,1,1,3,128]{4,2,3,1,0:T(1,128)S(1)}, s32[1,1,1,3,128]{4,2,3,1,0:T(1,128)}, u32[]{:S(2)}) copy-start(s32[1,1,1,3,128]{4,2,3,1,0:T(1,128)} %param.23) | copy-start | bytes 4612
  7.2 19.4 %copy-start.23 = (bf16[1,1,1,3,128]{4,3,2,1,0:T(4,128)(2,1)S(1)}, bf16[1,1,1,3,128]{4,3,2,1,0:T(4,128)(2,1)}, u32[]{:S(2)}) copy-start(bf16[1,1,1,3,128]{4,3,2,1,0:T(4,128)(2,1)} %param.22) | copy-start | bytes 2308
  9.9 20.8 %copy-start.58 = (s32[56]{0:T(128)S(1)}, s32[56]{0:T(128)}, u32[]{:S(2)}) copy-start(s32[56]{0:T(128)} %constant.259) | copy-start | bytes 676
  12.6 10.2 %collective-permute-start.1 = (bf16[1,2,2,7252]{3,2,1,0:T(2,128)(2,1)S(1)}, bf16[1,2,2,7252]{3,2,1,0:T(2,128)(2,1)S(1)}, u32[]{:S(2)}, u32[]{:S(2)}) collective-permute-start(bf16[1,2,2,7252]{3,2,1,0:T(2,128)(2,1)S(1)} %slice.445), channel_id=1, source_target_pairs={{4,0},{8,4},{12,8},{16,12},{20,16},{24,20},{28,24},{0,28},{5,1},{9... | collective-permute-start | bytes 174056 | tf_op jit(solution)/shard_map/ppermute | solution.py:30
  18.7 6.9 collective-permute-start
  26.1 1.4 collective-permute-start.3
  26.1 1.5 collective-permute-start.2
  28.7 13.6 %collective-permute-start.5 = (bf16[4,4,1,7252]{3,2,1,0:T(2,128)(2,1)S(1)}, bf16[4,4,1,7252]{3,2,1,0:T(2,128)(2,1)S(1)}, u32[]{:S(2)}, u32[]{:S(2)}) collective-permute-start(bf16[4,4,1,7252]{3,2,1,0:T(2,128)(2,1)S(1)} %get-tuple-element.302), channel_id=1, source_target_pairs={{1,0},{0,1},{3,2},{2,3},{5,4},{4,5},{7,6},{6,7},{9,8},{8,9},{11,10... | collective-permute-start | bytes 696200 | tf_op jit(solution)/shard_map/ppermute | solution.py:30
  30.3 21.4 %collective-permute-start.4 = (bf16[4,4,1,7252]{3,2,1,0:T(2,128)(2,1)S(1)}, bf16[4,4,1,7252]{3,2,1,0:T(2,128)(2,1)S(1)}, u32[]{:S(2)}, u32[]{:S(2)}) collective-permute-start(bf16[4,4,1,7252]{3,2,1,0:T(2,128)(2,1)S(1)} %get-tuple-element.301), channel_id=1, source_target_pairs={{0,1},{1,0},{2,3},{3,2},{4,5},{5,4},{6,7},{7,6},{8,9},{9,8},{10,11... | collective-permute-start | bytes 696200 | tf_op jit(solution)/shard_map/ppermute | solution.py:29
  30.8 25.3 %copy-start.29 = (s32[1024]{0:T(1024)}, s32[1024]{0:T(1024)S(1)}, u32[]{:S(2)}) copy-start(s32[1024]{0:T(1024)S(1)} %pad_clamp_fusion) | copy-start | bytes 12292
  31.7 26.2 %copy-start.20 = (bf16[913]{0:T(1024)(128)(2,1)}, bf16[913]{0:T(1024)(128)(2,1)S(1)}, u32[]{:S(2)}) copy-start(bf16[913]{0:T(1024)(128)(2,1)S(1)} %pad.59.clone) | copy-start | bytes 5482
  166.4 10.8 %copy-start.43 = (f32[128]{0:T(128)S(1)}, f32[128]{0:T(128)}, u32[]{:S(2)}) copy-start(f32[128]{0:T(128)} %get-tuple-element.343) | copy-start | bytes 1540
  166.4 10.8 %copy-start.44 = (f32[128]{0:T(128)S(1)}, f32[128]{0:T(128)}, u32[]{:S(2)}) copy-start(f32[128]{0:T(128)} %get-tuple-element.370) | copy-start | bytes 1540
  166.4 10.8 %copy-start.45 = (f32[128]{0:T(128)S(1)}, f32[128]{0:T(128)}, u32[]{:S(2)}) copy-start(f32[128]{0:T(128)} %get-tuple-element.337) | copy-start | bytes 1540
  166.4 10.8 %copy-start.46 = (f32[128]{0:T(128)S(1)}, f32[128]{0:T(128)}, u32[]{:S(2)}) copy-start(f32[128]{0:T(128)} %get-tuple-element.373) | copy-start | bytes 1540
  166.4 10.8 %copy-start.49 = (s32[128]{0:T(128)S(1)}, s32[128]{0:T(128)}, u32[]{:S(2)}) copy-start(s32[128]{0:T(128)} %get-tuple-element.348) | copy-start | bytes 1540
  166.5 10.8 %copy-start.50 = (s32[128]{0:T(128)S(1)}, s32[128]{0:T(128)}, u32[]{:S(2)}) copy-start(s32[128]{0:T(128)} %get-tuple-element.349) | copy-start | bytes 1540
  168.4 6.9 collective-permute-start.6
  169.4 7.0 collective-permute-start.7
  176.6 1.4 collective-permute-start.9
  176.6 1.5 collective-permute-start.8
  180.4 13.7 %collective-permute-start.11 = (bf16[4,4,1,7168]{3,2,1,0:T(2,128)(2,1)}, bf16[4,4,1,7168]{3,2,1,0:T(2,128)(2,1)}, u32[]{:S(2)}, u32[]{:S(2)}) collective-permute-start(bf16[4,4,1,7168]{3,2,1,0:T(2,128)(2,1)} %get-tuple-element.304), channel_id=1, source_target_pairs={{1,0},{0,1},{3,2},{2,3},{5,4},{4,5},{7,6},{6,7},{9,8},{8,9},{11,10... | collective-permute-start | bytes 688136 | tf_op jit(solution)/shard_map/ppermute | solution.py:30
  181.9 21.4 %collective-permute-start.10 = (bf16[4,4,1,7168]{3,2,1,0:T(2,128)(2,1)}, bf16[4,4,1,7168]{3,2,1,0:T(2,128)(2,1)}, u32[]{:S(2)}, u32[]{:S(2)}) collective-permute-start(bf16[4,4,1,7168]{3,2,1,0:T(2,128)(2,1)} %get-tuple-element.303), channel_id=1, source_target_pairs={{0,1},{1,0},{2,3},{3,2},{4,5},{5,4},{6,7},{7,6},{8,9},{9,8},{10,11... | collective-permute-start | bytes 688136 | tf_op jit(solution)/shard_map/ppermute | solution.py:29
  188.0 15.3 %copy-start.5 = (f32[128,4752]{0,1:T(8,128)}, f32[128,4752]{0,1:T(8,128)S(1)}, u32[]{:S(2)}) copy-start(f32[128,4752]{0,1:T(8,128)S(1)} %mul.1022) | copy-start | bytes 7299076
  327.1 17.2 %copy-start.2 = (f32[132,36,132]{2,0,1:T(8,128)}, f32[132,36,132]{2,0,1:T(8,128)S(1)}, u32[]{:S(2)}) copy-start(f32[132,36,132]{2,0,1:T(8,128)S(1)} %fusion.123) | copy-start | bytes 7527172
  327.1 10.7 %collective-permute-start.13 = (f32[132,2,132]{2,0,1:T(8,128)S(1)}, f32[132,2,132]{2,0,1:T(8,128)S(1)}, u32[]{:S(2)}, u32[]{:S(2)}) collective-permute-start(f32[132,2,132]{2,0,1:T(8,128)S(1)} %get-tuple-element.294), channel_id=1, source_target_pairs={{4,0},{8,4},{12,8},{16,12},{20,16},{24,20},{28,24},{0,28},{5,1},{9... | collective-permute-start | bytes 418184 | tf_op jit(solution)/shard_map/ppermute | solution.py:30
  332.2 10.5 %collective-permute-start.12 = (f32[132,2,132]{2,0,1:T(8,128)S(1)}, f32[132,2,132]{2,0,1:T(8,128)S(1)}, u32[]{:S(2)}, u32[]{:S(2)}) collective-permute-start(f32[132,2,132]{2,0,1:T(8,128)S(1)} %get-tuple-element.293), channel_id=1, source_target_pairs={{0,4},{4,8},{8,12},{12,16},{16,20},{20,24},{24,28},{28,0},{1,5},{5... | collective-permute-start | bytes 418184 | tf_op jit(solution)/shard_map/ppermute | solution.py:29
  342.8 1.3 collective-permute-start.15
  342.9 1.4 collective-permute-start.14
  351.7 5.0 collective-permute-start.17
  355.4 4.7 collective-permute-start.16
  386.5 4.6 collective-permute-start.18
  502.0 98.1 %all-to-all-start.1 = ((f32[8,1,131072]{2,1,0:T(1,128)}), f32[8,1,131072]{2,1,0:T(1,128)}, u32[]{:S(2)}, u32[]{:S(2)}) async-start(f32[8,1,131072]{2,1,0:T(1,128)} %reshape.1559), calls=%async_computation.1 | async-start | bytes 8388608 | tf_op jit(solution)/shard_map/all_to_all | solution.py:181
  506.9 429.6 %reduce-scatter.2.cloned.1.call-start = ((), (), s32[]{:S(2)}) async-start(), calls=%async_computation.5 | async-start | bytes 6291456 | tf_op jit(solution)/shard_map/reduce_scatter | solution.py:171
  938.6 8.6 collective-permute-start.19
  940.4 8.1 collective-permute-start.20
  948.6 1.3 collective-permute-start.22
  948.7 1.4 collective-permute-start.21
  956.4 11.8 %collective-permute-start.24 = (f32[132,36,2]{0,2,1:T(2,128)S(1)}, f32[132,36,2]{0,2,1:T(2,128)S(1)}, u32[]{:S(2)}, u32[]{:S(2)}) collective-permute-start(f32[132,36,2]{0,2,1:T(2,128)S(1)} %copy.237), channel_id=1, source_target_pairs={{1,0},{0,1},{3,2},{2,3},{5,4},{4,5},{7,6},{6,7},{9,8},{8,9},{11,10... | collective-permute-start | bytes 114056 | tf_op jit(solution)/shard_map/ppermute | solution.py:30
  961.0 9.5 collective-permute-start.23
  987.7 11.4 %copy-start.54 = (f32[128,2]{0,1:T(2,128)S(1)}, f32[128,2]{0,1:T(2,128)}, u32[]{:S(2)}) copy-start(f32[128,2]{0,1:T(2,128)} %fusion.147) | copy-start | bytes 3076
  987.7 11.4 %copy-start.56 = (f32[128,2]{0,1:T(2,128)S(1)}, f32[128,2]{0,1:T(2,128)}, u32[]{:S(2)}) copy-start(f32[128,2]{0,1:T(2,128)} %copy-done.55) | copy-start | bytes 3076
  987.7 11.9 %copy-start.11 = (f32[132,4752]{1,0:T(8,128)S(1)}, f32[132,4752]{1,0:T(8,128)}, u32[]{:S(2)}) copy-start(f32[132,4752]{1,0:T(8,128)} %reshape.1467) | copy-start | bytes 7527172
  987.7 11.9 %copy-start.35 = (f32[128]{0:T(128)S(1)}, f32[128]{0:T(128)}, u32[]{:S(2)}) copy-start(f32[128]{0:T(128)} %get-tuple-element.325) | copy-start | bytes 1540
  987.7 11.9 %copy-start.36 = (f32[128]{0:T(128)S(1)}, f32[128]{0:T(128)}, u32[]{:S(2)}) copy-start(f32[128]{0:T(128)} %get-tuple-element.366) | copy-start | bytes 1540
  987.7 11.9 %copy-start.37 = (f32[128]{0:T(128)S(1)}, f32[128]{0:T(128)}, u32[]{:S(2)}) copy-start(f32[128]{0:T(128)} %get-tuple-element.319) | copy-start | bytes 1540
  987.7 11.9 %copy-start.38 = (f32[128]{0:T(128)S(1)}, f32[128]{0:T(128)}, u32[]{:S(2)}) copy-start(f32[128]{0:T(128)} %get-tuple-element.369) | copy-start | bytes 1540
  (53 other events, 326.2 us)
Sparse Core Ops, SparseCore 0:
  925.7 10.7 reduce-scatter.1
where the time goes:
time: 1020 us
  local copies, waits for them, and re-layouts  322 us (32%)
  blocking collectives  198 us (19%)
  waiting for transfers between devices  160 us (16%)
  other arithmetic  156 us (15%)
  matrix products  126 us (12%)
  starting transfers between devices  36.7 us (4%)
  between operations  15.6 us (2%)
    all_to_all x2, blocking collectives, across_gz(): return lax.all_to_all(blocks, 'gz', split_axis=0, concat_axis=0, tiled=True)  101 us
    dot_general x17, matrix products, product(): jnp.dot(left, right, precision=HIGHEST_PRECISION, preferred_element_type=...  98.1 us
    all_to_all x1, blocking collectives, across_gx(): return lax.all_to_all(blocks, 'gx', split_axis=0, concat_axis=0, tiled=True)  97.3 us
    all_to_all x1, waiting for transfers between devices, across_gx(): return lax.all_to_all(blocks, 'gx', split_axis=0, concat_axis=0, tiled=True)  91.9 us
    unnamed x124, local copies, waits for them, and re-layouts  40.5 us
    ppermute x12, waiting for transfers between devices, extended_2(): before = lax.ppermute(last, axis, up)  31.8 us
    all_to_all x2, other arithmetic, across_gx(): return lax.all_to_all(blocks, 'gx', split_axis=0, concat_axis=0, tiled=True)  28.1 us
    ppermute x12, starting transfers between devices, extended_2(): after = lax.ppermute(leading, axis, down)  25.6 us
  transfers between devices with their start and end apart: 27, of which 22 were waited for; matrix products, arithmetic and copies ran while one was open for 4% of the time, Pallas kernels for 0%

commit v1 on v0

v1 whole, which is shorter than its diff:
```python
import math

import jax
import jax.numpy as jnp
import numpy as np
from jax import lax
from jax.experimental import pallas as pl
from jax.experimental.pallas import tpu as pltpu
from jax.sharding import PartitionSpec as P

C = 128
NB = 8
LAYERS = 2
NEIGH = 16
ENV = 7
MESH = 256


COULOMB = 4.0
EWALD = 0.7
HIGHEST_PRECISION = lax.Precision.HIGHEST


def outer_cells():
    found = []
    for first in range(4):
        for second in range(4):
            for third in range(4):
                if 0 < first < 3 and 0 < second < 3 and (0 < third < 3):
                    continue
                found.append((first, second, third))
    return found


def offset_of(coord):
    return -1 if coord == 0 else 1 if coord == 3 else 0


def spline(fraction_in):
    lower_t = 1.0 - fraction_in
    weights = jnp.stack(
        [
            lower_t * lower_t * lower_t / 6.0,
            (3.0 * fraction_in * fraction_in * fraction_in - 6.0 * fraction_in * fraction_in + 4.0)
            / 6.0,
            (
                -3.0 * fraction_in * fraction_in * fraction_in
                + 3.0 * fraction_in * fraction_in
                + 3.0 * fraction_in
                + 1.0
            )
            / 6.0,
            fraction_in * fraction_in * fraction_in / 6.0,
        ]
    )
    slopes = jnp.stack(
        [
            -0.5 * lower_t * lower_t,
            0.5 * (3.0 * fraction_in * fraction_in - 4.0 * fraction_in),
            0.5 * (-3.0 * fraction_in * fraction_in + 2.0 * fraction_in + 1.0),
            0.5 * fraction_in * fraction_in,
        ]
    )
    return (weights, slopes)


def frequency(waves):
    signed = jnp.where(waves <= MESH // 2, waves, waves - MESH).astype(jnp.float32) / MESH
    modulus = 9.0 / jnp.square(2.0 + jnp.cos(waves.astype(jnp.float32) * (2.0 * math.pi / MESH)))
    return (signed, modulus)


def influence(wave_y, wave_z, wave_x):
    freq_y, modul_y = frequency(wave_y)
    freq_z, modul_z = frequency(wave_z)
    freq_x, modul_x = frequency(wave_x)
    wave_square = (
        jnp.square(freq_x)[None, None, :]
        + jnp.square(freq_y)[:, None, None]
        + jnp.square(freq_z)[None, :, None]
    )
    positive = wave_square > 0.0
    gaussian = jnp.exp(-(math.pi * math.pi / (EWALD * EWALD)) * wave_square)
    kernel = jnp.where(positive, gaussian / jnp.where(positive, wave_square, 1.0), 0.0)
    moduli = modul_x[None, None, :] * modul_y[:, None, None] * modul_z[None, :, None]
    return kernel * moduli * (COULOMB / (math.pi * MESH**3))


def phases(left, right):
    turns = left[:, None] * right[None, :] % MESH
    angle = turns.astype(jnp.float32) * (2.0 * math.pi / MESH)
    return (jnp.cos(angle), jnp.sin(angle))


AXES = ("gx", "gy", "gz")


def source_of(coord):
    return 1 if coord == 0 else 0 if coord == 3 else coord - 1


def layer_kernel(
    ids, links, feats, geo, own, own_geo, radial_in, radial_out, mix_weight, out, s_acc, v_acc
):
    step = pl.program_id(0)
    atom_count = own.shape[0]

    @pl.when(step == 0)
    def _():
        s_acc[...] = jnp.zeros_like(s_acc)
        v_acc[...] = jnp.zeros_like(v_acc)

    picked = (links[...] == ids[...]).astype(jnp.float32).astype(jnp.bfloat16)
    rows = jnp.dot(picked, feats[...], preferred_element_type=jnp.float32)
    spots = jnp.dot(picked, geo[...], preferred_element_type=jnp.float32)
    edges = rows.shape[0]
    slots = edges // atom_count
    here = own_geo[...].astype(jnp.float32)
    located = jnp.concatenate([here[:, 0:3] + here[:, 3:6]] * slots, axis=0)
    displace = spots[:, 0:3] + spots[:, 3:6] - located
    length_sq = jnp.sum(displace * displace, axis=1, keepdims=True)
    distance = jnp.sqrt(length_sq)
    direction = displace / jnp.sqrt(length_sq + 1.0)
    spacing = ENV / (NB - 1)
    centres = lax.broadcasted_iota(jnp.int32, (edges, C), 1).astype(jnp.float32) * spacing
    envelope = jnp.square(jnp.maximum(1.0 - length_sq / (ENV * ENV), 0.0))
    basis = jnp.exp(-jnp.square((distance - centres) / spacing)) * envelope
    hidden = jnp.dot(
        basis.astype(jnp.bfloat16), radial_in[...], preferred_element_type=jnp.float32
    )
    hidden = (hidden / (1.0 + jnp.exp(-hidden))).astype(jnp.bfloat16)
    radial = jnp.dot(hidden, radial_out[...], preferred_element_type=jnp.float32)
    scalars = rows[:, :C]
    units = [direction[:, d : d + 1] for d in range(3)]
    vectors = [rows[:, C * (d + 1) : C * (d + 2)] for d in range(3)]
    projected = units[0] * vectors[0] + units[1] * vectors[1] + units[2] * vectors[2]
    scaled = radial[:, 2 * C : 3 * C] * scalars
    fourth = radial[:, 3 * C :]

    def over_slots(edge_values):
        return sum(edge_values[k * atom_count : (k + 1) * atom_count] for k in range(slots))

    s_acc[...] += over_slots(radial[:, :C] * scalars + radial[:, C : 2 * C] * projected)
    for d in range(3):
        v_acc[d] += over_slots(units[d] * scaled + fourth * vectors[d])

    @pl.when(step == pl.num_programs(0) - 1)
    def _():
        inverse_root = 1.0 / math.sqrt(NEIGH)
        previous = own[...].astype(jnp.float32)
        message = (s_acc[...] * inverse_root).astype(jnp.bfloat16)
        mixed = jnp.dot(message, mix_weight[0], preferred_element_type=jnp.float32)
        out[:, :C] = (previous[:, :C] + mixed / (1.0 + jnp.exp(-mixed))).astype(jnp.bfloat16)
        for d in range(3):
            message = (v_acc[d] * inverse_root).astype(jnp.bfloat16)
            mixed = jnp.dot(message, mix_weight[1], preferred_element_type=jnp.float32)
            span = slice(C * (d + 1), C * (d + 2))
            out[:, span] = (previous[:, span] + mixed).astype(jnp.bfloat16)


def layer(ids, links, feats, geo, own, own_geo, radial_in, radial_out, mix_weight):
    atom_count = own.shape[0]
    edge_block = 4 * atom_count
    whole = lambda array: pl.BlockSpec(array.shape, lambda i: (0,) * array.ndim)
    return pl.pallas_call(
        layer_kernel,
        grid=(links.shape[0] // edge_block,),
        out_shape=jax.ShapeDtypeStruct(own.shape, jnp.bfloat16),
        in_specs=[
            whole(ids),
            pl.BlockSpec((edge_block, 1), lambda i: (i, 0)),
            whole(feats),
            whole(geo),
            whole(own),
            whole(own_geo),
            whole(radial_in),
            whole(radial_out),
            whole(mix_weight),
        ],
        out_specs=pl.BlockSpec(own.shape, lambda i: (0, 0)),
        scratch_shapes=[
            pltpu.VMEM((atom_count, C), jnp.float32),
            pltpu.VMEM((3, atom_count, C), jnp.float32),
        ],
        compiler_params=pltpu.CompilerParams(
            dimension_semantics=("arbitrary",), vmem_limit_bytes=40 * 1024 * 1024
        ),
    )(ids, links, feats, geo, own, own_geo, radial_in, radial_out, mix_weight)


def ghost_plan(counts):
    groups = {}
    for number, corner in enumerate(outer_cells()):
        offset = tuple(offset_of(coord) for coord in corner)
        bits = [source_of(coord) for coord in corner]
        octant = 4 * bits[0] + 2 * bits[1] + bits[2]
        key = tuple(o % n for o, n in zip(offset, counts))
        groups.setdefault(key, []).append((number, octant, offset))
    return groups


def exchange(buffers, counts, groups):
    pieces = []
    devices = list(np.ndindex(*counts))
    linear = lambda spot: (spot[0] * counts[1] + spot[1]) * counts[2] + spot[2]
    for key, members in groups.items():
        octants = [member[1] for member in members]
        if octants == list(range(8)):
            block = buffers
        else:
            block = jnp.concatenate([buffers[o : o + 1] for o in octants], axis=0)
        if any(key):
            route = []
            for spot in devices:
                source = tuple((a + o) % n for a, o, n in zip(spot, key, counts))
                route.append((linear(source), linear(spot)))
            block = lax.ppermute(block, AXES, route)
        pieces.append(block)
    return jnp.concatenate(pieces, axis=0)


def cas_table(left, right):
    cosine, sine = phases(left, right)
    return cosine + sine


def local_rows(coefficient, first, span):
    slot_index = jnp.arange(span, dtype=jnp.int32)[None, :, None]
    summed = 0.0
    for offset in range(4):
        summed = summed + jnp.where(
            slot_index == ((first + offset) % MESH)[:, None, :], coefficient[offset][:, None, :], 0.0
        )
    return summed


def mm(pattern, left, right):
    return jnp.einsum(
        pattern, left, right, precision=lax.Precision.HIGH, preferred_element_type=jnp.float32
    )


def per_device(
    features,
    fraction,
    cell_index,
    species,
    octant_rows,
    neighbours,
    radial_in,
    radial_out,
    mix_weight,
    readout,
    species_table,
):
    bf16 = jnp.bfloat16
    current = features[0, 0, 0]
    fraction_here = fraction[0, 0, 0]
    cells_here = cell_index[0, 0, 0]
    kinds = species[0, 0, 0]
    chosen_rows = octant_rows[0, 0, 0].reshape(-1)
    links = neighbours[0, 0, 0].reshape(-1, 1)
    atom_count, feat_width = current.shape
    ghost_count = chosen_rows.shape[0] // 8
    counts = tuple(lax.axis_size(axis) for axis in AXES)
    count_x, count_y, count_z = counts
    total = count_x * count_y * count_z
    span_x, span_y, span_z = (MESH // n for n in counts)
    small = jnp.concatenate([cells_here.astype(bf16), fraction_here], axis=0)
    everyone = lax.all_gather(small, AXES, axis=0, tiled=False)
    own_geo = jnp.pad(jnp.transpose(small), ((0, 0), (0, C - 6)))
    pick = (chosen_rows[:, None] == jnp.arange(atom_count, dtype=jnp.int32)[None, :]).astype(bf16)
    groups = ghost_plan(counts)
    ids = list(range(atom_count))
    shift_rows = []
    for members in groups.values():
        for number, _, offset in members:
            ids += [atom_count + number * ghost_count + r for r in range(ghost_count)]
            shift = [o * w for o, w in zip(offset, (span_x, span_y, span_z))]
            shift_rows += [shift] * ghost_count
    real_rows = len(ids)
    table_rows = -(-real_rows // 128) * 128
    ids = jnp.asarray(np.array(ids + [-1] * (table_rows - real_rows), np.int32))[None, :]
    shift_rows = np.pad(np.array(shift_rows, np.float32), ((0, 0), (0, C - 3)))
    fill = table_rows - real_rows

    def outgoing(values):
        return jnp.dot(pick, values, preferred_element_type=jnp.float32).astype(bf16).reshape(
            8, ghost_count, -1
        )

    geo = own_geo
    for index in range(LAYERS):
        values = jnp.concatenate([current, own_geo], axis=1) if index == 0 else current
        arrived = exchange(outgoing(values), counts, groups).reshape(
            real_rows - atom_count, values.shape[1]
        )
        feats = jnp.concatenate(
            [current, arrived[:, :feat_width], jnp.zeros((fill, feat_width), bf16)], axis=0
        )
        if index == 0:
            ghost_geo = (arrived[:, feat_width:].astype(jnp.float32) + shift_rows).astype(bf16)
            geo = jnp.concatenate([own_geo, ghost_geo, jnp.zeros((fill, C), bf16)], axis=0)
        first_pad = jnp.pad(radial_in[index], ((0, C - NB), (0, C - radial_in.shape[2])))
        second_pad = jnp.pad(radial_out[index], ((0, C - radial_out.shape[1]), (0, 0)))
        current = layer(
            ids, links, feats, geo, current, own_geo, first_pad, second_pad, mix_weight[index]
        )

    head_out = jnp.dot(current[:, :C], readout, preferred_element_type=jnp.float32)
    one_hot = (
        kinds[:, None] == jnp.arange(species_table.shape[0], dtype=jnp.int32)[None, :]
    ).astype(jnp.float32)
    species_term = jnp.dot(
        one_hot, species_table, precision=HIGHEST_PRECISION, preferred_element_type=jnp.float32
    )
    base_energy = head_out[:, 0] + species_term[:, 0]
    charge = head_out[:, 1] + species_term[:, 1]
    charges = lax.all_gather(charge, AXES, axis=0, tiled=False).reshape(count_x, -1)

    device = (lax.axis_index("gx") * count_y + lax.axis_index("gy")) * count_z
    device = device + lax.axis_index("gz")
    wave_count = MESH // total
    waves_y = device * wave_count + jnp.arange(wave_count, dtype=jnp.int32)
    full = jnp.arange(MESH, dtype=jnp.int32)
    table = everyone.reshape(count_x, count_y * count_z, 6, atom_count)
    table = jnp.transpose(table, (2, 0, 1, 3)).reshape(6, count_x, -1).astype(jnp.float32)
    all_cells = table[:3].astype(jnp.int32)
    weights, slopes = spline(table[3:])
    order = jnp.arange(count_y * count_z * atom_count, dtype=jnp.int32) // atom_count
    start_y = (order // count_z * span_y)[None, :]
    start_z = (order % count_z * span_z)[None, :]
    width_x = -(-(span_x + 3) // 8) * 8
    weight_x = local_rows(weights[:, 0], all_cells[0], width_x)
    slope_x = local_rows(slopes[:, 0], all_cells[0], width_x)
    first_z = all_cells[2] + start_z + (MESH - 1)
    weight_z = local_rows(weights[:, 2], first_z, MESH)
    slope_z = local_rows(slopes[:, 2], first_z, MESH)
    place_y = all_cells[1] + start_y
    turns = (waves_y[:, None, None] * place_y[None]) % MESH
    angle = turns.astype(jnp.float32) * (2.0 * math.pi / MESH)
    cosine_y, sine_y = jnp.cos(angle), jnp.sin(angle)
    step_cosine, step_sine = phases(waves_y, jnp.arange(4, dtype=jnp.int32) - 1 + MESH)
    plus, minus = step_cosine + step_sine, step_cosine - step_sine

    def along_y(values):
        first = sum(plus[:, m][:, None, None] * values[m][None] for m in range(4))
        second = sum(minus[:, m][:, None, None] * values[m][None] for m in range(4))
        return cosine_y * first + sine_y * second

    weight_y = along_y(weights[:, 1])
    slope_y = along_y(slopes[:, 1])
    slots_x = (
        jnp.arange(count_x, dtype=jnp.int32)[:, None] * span_x
        + jnp.arange(width_x, dtype=jnp.int32)[None, :]
        + (MESH - 1)
    ).reshape(-1) % MESH
    cas_x = cas_table(full, slots_x).reshape(MESH, count_x, width_x)
    cas_z = cas_table(full, full)
    influence_here = influence(waves_y, full, full)

    loaded = (jnp.transpose(weight_y, (1, 0, 2)) * charges[:, None, :])[:, :, None, :]
    loaded = loaded * weight_x[:, None, :, :]
    spread = mm("ikxa,iza->ikxz", loaded, weight_z)
    spectrum = mm("ikxz,zw->ikxw", spread, cas_z)
    spectrum = mm("vix,ikxw->kwv", cas_x, spectrum) * influence_here
    back = mm("vix,kwv->ikxw", cas_x, spectrum)
    back = mm("ikxw,wz->ikxz", back, cas_z)
    level = mm("ikxz,iza->ikxa", back, weight_z)
    level_slope = mm("ikxz,iza->ikxa", back, slope_z)
    by_x = jnp.transpose(jnp.sum(level * weight_x[:, None], axis=2), (1, 0, 2))
    by_slope_x = jnp.transpose(jnp.sum(level * slope_x[:, None], axis=2), (1, 0, 2))
    by_slope_z = jnp.transpose(jnp.sum(level_slope * weight_x[:, None], axis=2), (1, 0, 2))
    partial = jnp.stack(
        [
            jnp.sum(weight_y * by_x, axis=0),
            jnp.sum(weight_y * by_slope_x, axis=0),
            jnp.sum(slope_y * by_x, axis=0),
            jnp.sum(weight_y * by_slope_z, axis=0),
        ]
    )
    partial = jnp.transpose(partial.reshape(4, total, atom_count), (1, 0, 2))
    mine = lax.psum_scatter(partial, AXES, scatter_dimension=0, tiled=False)
    recip_force = -charge[None, :] * mine[1:]
    site_energy = base_energy + 0.5 * charge * mine[0]
    return (current[None, None, None], site_energy[None, None, None], recip_force[None, None, None])


def solution(mesh):
    in_specs = (
        P("gx", "gy", "gz", None, None),
        P("gx", "gy", "gz", None, None),
        P("gx", "gy", "gz", None, None),
        P("gx", "gy", "gz", None),
        P("gx", "gy", "gz", None, None),
        P("gx", "gy", "gz", None, None),
        P(),
        P(),
        P(),
        P(),
        P(),
    )
    out_specs = (
        P("gx", "gy", "gz", None, None),
        P("gx", "gy", "gz", None),
        P("gx", "gy", "gz", None, None),
    )
    return jax.shard_map(
        per_device, mesh=mesh, in_specs=in_specs, out_specs=out_specs, check_vma=False
    )
```

time: 1020 us -> 377 us (0.37)
  local copies, waits for them, and re-layouts: 322 us -> 24.2 us
  other arithmetic: 156 us -> 11.7 us
  matrix products: 126 us -> 29.9 us
  blocking collectives: 198 us -> 133 us
  waiting for transfers between devices: 160 us -> 124 us
  Pallas kernels: 0 us -> 17.1 us
  starting transfers between devices: 36.7 us -> 20.9 us
    all_to_all x3 -> x0, blocking collectives: 198 us -> none  [the longest x2 101 us: across_gz(): return lax.all_to_all(blocks, 'gz', split_axis=0, concat_axis=0, tiled=True)]
    all_gather x0 -> x2, blocking collectives: none -> 133 us  [the longest x1 67.6 us: per_device(): everyone = lax.all_gather(small, AXES, axis=0, tiled=False)]
    unnamed x1 -> x2, waiting for transfers between devices: 0.02 us -> 114 us
    dot_general x37 -> x9, matrix products: 124 us -> 28.2 us  [the longest x7 26.8 us: mm(): jnp.einsum(pattern, left, right, precision=lax.Precision.HIGH, preferred_...]
    all_to_all x1 -> x0, waiting for transfers between devices: 91.9 us -> none  [across_gx(): return lax.all_to_all(blocks, 'gx', split_axis=0, concat_axis=0, tiled=True)]
    gather x18 -> x0, local copies, waits for them, and re-layouts: 51.6 us -> none  [the longest x8 24.7 us: interact(): displace = places[links] - located[None]]
    ppermute x25 -> x22, waiting for transfers between devices: 56.7 us -> 10 us  [exchange(): block = lax.ppermute(block, AXES, route)]
    reduce_sum x16 -> x2, other arithmetic: 34.2 us -> 1.53 us  [the longest x1 0.8 us: per_device(): jnp.sum(weight_y * by_x, axis=0)]
  transfers between devices with their start and end apart: 27 -> 23, of which waited for: 22 -> 5; matrix products, arithmetic and copies ran while one was open for 4% -> 6% of each run, Pallas kernels for 0% -> 0%
where the time goes in v1:
time: 377 us; the launch traced here: 376 us
  blocking collectives  133 us (35%)
  waiting for transfers between devices  124 us (33%)
  matrix products  29.9 us (8%)
  local copies, waits for them, and re-layouts  24.2 us (6%)
  starting transfers between devices  20.9 us (6%)
  Pallas kernels  17.1 us (5%)
  between operations  15.3 us (4%)
  other arithmetic  11.7 us (3%)
    unnamed x2, waiting for transfers between devices  114 us
    all_gather x1, blocking collectives, per_device(): everyone = lax.all_gather(small, AXES, axis=0, tiled=False)  67.6 us
    all_gather x1, blocking collectives, per_device(): lax.all_gather(charge, AXES, axis=0, tiled=False).reshape(count_x, -1)  65.4 us
    dot_general x7, matrix products, mm(): jnp.einsum(pattern, left, right, precision=lax.Precision.HIGH, preferred_...  26.8 us
    ppermute x22, starting transfers between devices, exchange(): block = lax.ppermute(block, AXES, route)  20.9 us
    pallas_call x2, Pallas kernels, layer(): pl.pallas_call(layer_kernel, grid=(links.shape[0] // edge_block,), out_sh...  17.1 us
    unnamed x148, local copies, waits for them, and re-layouts  14.7 us
    ppermute x22, waiting for transfers between devices, exchange(): block = lax.ppermute(block, AXES, route)  10 us
  transfers between devices with their start and end apart: 23, of which 5 were waited for; matrix products, arithmetic and copies ran while one was open for 6% of the time, Pallas kernels for 0%

profile of v1, /device:TPU:0, one launch (start us, length us, event | category | flops | bytes accessed | tf_op | source)
XLA Modules:
  0.0 375.6 jit_solution(12552963967264564001)
XLA Ops:
  7.3 0.8 fusion.150
  8.0 0.7 fusion.186
  8.8 0.8 eq.116
  9.6 1.1 convolution_convert_fusion
  10.9 3.4 collective-permute-start
  14.3 1.8 collective-permute-start.1
  16.1 1.4 collective-permute-start.2
  17.5 1.5 collective-permute-start.3
  20.0 1.1 copy.48.links
  21.2 67.6 %all-gather.2 = bf16[32,6,128]{2,1,0:T(8,128)(2,1)S(1)} all-gather(bf16[1,6,128]{2,1,0:T(8,128)(2,1)S(1)} %get-tuple-element.146), channel_id=2, replica_groups=mesh['gx'=8,'gy'=2,'gz'=2] {'gx','gy','gz'}, dimensions={0}, use_global_device_ids=true | all-gather | bytes 50688 | tf_op jit(solution)/shard_map/all_gather | solution.py:270
  89.0 0.7 add_select_fusion.14
  91.6 0.8 fusion.102
  95.1 0.7 add_select_fusion.9
  95.8 1.6 select_add_fusion.3
  100.1 0.7 constant_dynamic-update-slice_fusion.30
  101.2 0.7 constant_dynamic-update-slice_fusion.29
  101.9 6.1 %collective-permute-done.6 = bf16[8,14,640]{2,1,0:T(8,128)(2,1)S(1)} collective-permute-done((bf16[8,14,640]{2,1,0:T(8,128)(2,1)S(1)}, bf16[8,14,640]{2,1,0:T(8,128)(2,1)S(1)}, u32[]{:S(2)}, u32[]{:S(2)}) %collective-permute-start.6) | collective-permute-done | bytes 143392 | tf_op jit(solution)/shard_map/ppermute | solution.py:217
  108.0 0.7 constant_dynamic-update-slice_fusion.28
  111.2 1.4 reshape.696
  113.3 8.2 %shard_map.148.own = bf16[128,512]{1,0:T(8,128)(2,1)S(1)} custom-call(s32[1,1024]{1,0:T(1,128)S(1)} %copy-done.2, s32[2048,1]{1,0:T(8,128)S(1)} %copy.48.links, bf16[1024,512]{1,0:T(8,128)(2,1)S(1)} %maximum_maximum_fusion.feats, bf16[1024,128]{1,0:T(8,128)(2,1)S(1)} %maximum_maximum_fusion.2.geo, bf16[128,512]{1,0:T(8,128)(2,1)S(1)} %bitcast.354, ...), custom_call_target="tpu_custom_call" | custom-call | tf_op jit(solution)/shard_map/pallas_call | solution.py:165
  122.4 2.1 collective-permute-start.12
  124.5 1.3 collective-permute-start.13
  125.8 0.7 collective-permute-start.14
  126.8 0.8 collective-permute-start.15
  127.6 2.1 collective-permute-done.11
  130.3 0.8 collective-permute-start.17
  131.7 1.5 collective-permute-done.13
  133.1 1.8 collective-permute-start.18
  135.6 0.7 collective-permute-start.19
  136.9 2.3 collective-permute-start.20
  139.2 0.7 constant_dynamic-update-slice_fusion.65
  139.9 0.7 collective-permute-start.21
  144.8 1.3 reshape.697
  146.6 8.9 %shard_map.149 = bf16[128,512]{1,0:T(8,128)(2,1)} custom-call(s32[1,1024]{1,0:T(1,128)S(1)} %copy-done.2, s32[2048,1]{1,0:T(8,128)S(1)} %copy.48.links, bf16[1024,512]{1,0:T(8,128)(2,1)S(1)} %maximum_maximum_fusion.1.feats, bf16[1024,128]{1,0:T(8,128)(2,1)S(1)} %maximum_maximum_fusion.2.geo, bf16[128,512]{1,0:T(8,128)(2,1)S(1)} %shard_map.148.own, ...), custom_call_target="tpu_custom_call" | custom-call | tf_op jit(solution)/shard_map/pallas_call | solution.py:165
  155.5 0.9 fusion.124
  156.4 65.4 %all-gather.1 = f32[4096,1]{0,1:T(1,128)S(1)} all-gather(f32[128,1]{0,1:T(1,128)S(1)} %get-tuple-element.16), channel_id=3, replica_groups=mesh['gx'=8,'gy'=2,'gz'=2] {'gx','gy','gz'}, dimensions={0}, use_global_device_ids=true | all-gather | bytes 16896 | tf_op jit(solution)/shard_map/all_gather | solution.py:319
  222.3 0.7 reduce.3
  223.9 4.5 %fusion = f32[8,8,40,256]{3,2,1,0:T(8,128)S(1)} fusion(f32[8,40,512]{2,1,0:T(8,128)S(1)} %copy-done.3, f32[8,8,512]{2,1,0:T(8,128)S(1)} %copy.50, f32[8,512]{1,0:T(8,128)S(1)} %copy-done.14, s32[8,512]{1,0:T(8,128)S(1)} %copy-done.21, f32[8,512]{1,0:T(8,128)S(1)} %copy-done.15, s32[8,512]{1,0:T(8,128)S(1)} %copy-done.20, f32[8,512]{1,0:T(8,128)S(1)} %copy-done.16, ...), kind=kOutput, calls=%fused_computation.3 | convolution fusion | flops 2026110976 | bytes 3538944 | tf_op jit(solution)/shard_map/ikxa,iza->ikxz/dot_general | solution.py:238
  228.5 2.2 fusion.80
  230.8 3.9 %fusion.71 = f32[8,256,256,1]{2,1,0,3:T(8,128)S(1)} fusion(f32[8,8,40,256]{3,2,1,0:T(8,128)S(1)} %fusion.80, s32[8,40]{1,0:T(8,128)S(1)} %copy-done.42), kind=kOutput, calls=%fused_computation.95 | convolution fusion | flops 1007861760 | bytes 4719872 | tf_op jit(solution)/shard_map/vix,ikxw->kwv/dot_general | solution.py:238
  234.7 3.6 fusion.23
  238.4 2.3 fusion.14
  240.7 5.7 %multiply_reduce_fusion.1 = (f32[8,8,512]{2,1,0:T(8,128)S(1)}, f32[8,8,512]{2,1,0:T(8,128)S(1)}) fusion(f32[8,40,512]{2,1,0:T(8,128)S(1)} %copy-done.4, f32[8,40,512]{2,1,0:T(8,128)S(1)} %copy-done.3, f32[8,8,40,256]{3,2,1,0:T(8,128)S(1)} %fusion.14, f32[8,512]{1,0:T(8,128)S(1)} %copy-done.14, s32[8,512]{1,0:T(8,128)S(1)} %copy-done.21, ...), kind=kOutput, calls=%fused_computation.1 | convolution fusion | flops 2029977600 | bytes 4325376 | tf_op jit(solution)/shard_map/ikxz,iza->ikxa/dot_general | solution.py:238
  246.5 4.6 %multiply_reduce_fusion = f32[8,8,512]{2,1,0:T(8,128)S(1)} fusion(f32[8,40,512]{2,1,0:T(8,128)S(1)} %copy-done.3, f32[8,8,40,256]{3,2,1,0:T(8,128)S(1)} %fusion.14, f32[8,512]{1,0:T(8,128)S(1)} %get-tuple-element.103, f32[8,512]{1,0:T(8,128)S(1)} %get-tuple-element.151, f32[8,512]{1,0:T(8,128)S(1)} %copy-done.12, f32[8,512]{1,0:T(8,128)S(1)} %copy-done.13, ...), kind=kOutput, calls=%fused_computation | convolution fusion | flops 2027388928 | bytes 3538944 | tf_op jit(solution)/shard_map/ikxz,iza->ikxa/dot_general | solution.py:238
  251.1 0.7 fusion.95
  251.9 0.8 fusion.96
  252.8 0.7 maximum_bitcast_fusion
  253.5 113.5 %all-reduce.8.cloned.1.call-done = f32[32,4,128]{2,1,0:T(4,128)} async-done(((f32[32,4,128]{2,1,0:T(4,128)}), f32[32,4,128]{2,1,0:T(4,128)}) %all-reduce.8.cloned.1.call-update) | async-done | bytes 65552
  (234 shorter events, 23.5 us)
Async XLA Ops:
  7.2 84.4 %copy-start = (f32[2,2]{1,0:T(2,128)S(1)}, f32[2,2]{1,0:T(2,128)}, u32[]{:S(2)}) copy-start(f32[2,2]{1,0:T(2,128)} %param.23) | copy-start | bytes 52
  7.2 359.8 %all-reduce.8.cloned.1.call-start = ((), (), s32[]{:S(2)}) async-start(), calls=%async_computation | async-start | bytes 131072
  10.8 80.8 %copy-start.48 = (s32[1,1,1,128]{3,2,1,0:T(1,128)S(1)}, s32[1,1,1,128]{3,2,1,0:T(1,128)}, u32[]{:S(2)}) copy-start(s32[1,1,1,128]{3,2,1,0:T(1,128)} %param.16) | copy-start | bytes 1540
  10.9 86.6 %collective-permute-start = (bf16[4,14,640]{2,1,0:T(8,128)(2,1)S(1)}, bf16[4,14,640]{2,1,0:T(8,128)(2,1)S(1)}, u32[]{:S(2)}, u32[]{:S(2)}) collective-permute-start(bf16[4,14,640]{2,1,0:T(8,128)(2,1)S(1)} %get-tuple-element.82), channel_id=1, source_target_pairs={{31,0},{30,1},{29,2},{28,3},{3,4},{2,5},{1,6},{0,7},{7,8},{6,9},{5... | collective-permute-start | bytes 215048 | tf_op jit(solution)/shard_map/ppermute | solution.py:217
  14.3 83.9 %collective-permute-start.1 = (bf16[4,14,640]{2,1,0:T(8,128)(2,1)S(1)}, bf16[4,14,640]{2,1,0:T(8,128)(2,1)S(1)}, u32[]{:S(2)}, u32[]{:S(2)}) collective-permute-start(bf16[4,14,640]{2,1,0:T(8,128)(2,1)S(1)} %get-tuple-element.81), channel_id=1, source_target_pairs={{30,0},{31,1},{28,2},{29,3},{2,4},{3,5},{0,6},{1,7},{6,8},{7,9},{4... | collective-permute-start | bytes 215048 | tf_op jit(solution)/shard_map/ppermute | solution.py:217
  16.1 82.8 %collective-permute-start.2 = (bf16[4,14,640]{2,1,0:T(8,128)(2,1)S(1)}, bf16[4,14,640]{2,1,0:T(8,128)(2,1)S(1)}, u32[]{:S(2)}, u32[]{:S(2)}) collective-permute-start(bf16[4,14,640]{2,1,0:T(8,128)(2,1)S(1)} %get-tuple-element.80), channel_id=1, source_target_pairs={{29,0},{28,1},{31,2},{30,3},{1,4},{0,5},{3,6},{2,7},{5,8},{4,9},{7... | collective-permute-start | bytes 215048 | tf_op jit(solution)/shard_map/ppermute | solution.py:217
  17.5 82.0 %collective-permute-start.3 = (bf16[4,14,640]{2,1,0:T(8,128)(2,1)S(1)}, bf16[4,14,640]{2,1,0:T(8,128)(2,1)S(1)}, u32[]{:S(2)}, u32[]{:S(2)}) collective-permute-start(bf16[4,14,640]{2,1,0:T(8,128)(2,1)S(1)} %get-tuple-element.79), channel_id=1, source_target_pairs={{28,0},{29,1},{30,2},{31,3},{0,4},{1,5},{2,6},{3,7},{4,8},{5,9},{6... | collective-permute-start | bytes 215048 | tf_op jit(solution)/shard_map/ppermute | solution.py:217
  19.4 80.8 %collective-permute-start.4 = (bf16[8,14,640]{2,1,0:T(8,128)(2,1)S(1)}, bf16[8,14,640]{2,1,0:T(8,128)(2,1)S(1)}, u32[]{:S(2)}, u32[]{:S(2)}) collective-permute-start(bf16[8,14,640]{2,1,0:T(8,128)(2,1)S(1)} %get-tuple-element.36), channel_id=1, source_target_pairs={{3,0},{2,1},{1,2},{0,3},{7,4},{6,5},{5,6},{4,7},{11,8},{10,9},{9,1... | collective-permute-start | bytes 430088 | tf_op jit(solution)/shard_map/ppermute | solution.py:217
  19.9 77.5 %copy-start.38 = (f32[256]{0:T(256)}, f32[256]{0:T(256)S(1)}, u32[]{:S(2)}) copy-start(f32[256]{0:T(256)S(1)} %get-tuple-element.172) | copy-start | bytes 3076
  19.9 77.5 %copy-start.40 = (f32[256]{0:T(256)}, f32[256]{0:T(256)S(1)}, u32[]{:S(2)}) copy-start(f32[256]{0:T(256)S(1)} %get-tuple-element.173) | copy-start | bytes 3076
  97.5 3.3 collective-permute-start.5
  98.2 9.8 %collective-permute-start.6 = (bf16[8,14,640]{2,1,0:T(8,128)(2,1)S(1)}, bf16[8,14,640]{2,1,0:T(8,128)(2,1)S(1)}, u32[]{:S(2)}, u32[]{:S(2)}) collective-permute-start(bf16[8,14,640]{2,1,0:T(8,128)(2,1)S(1)} %get-tuple-element.25), channel_id=1, source_target_pairs={{1,0},{0,1},{3,2},{2,3},{5,4},{4,5},{7,6},{6,7},{9,8},{8,9},{11,10... | collective-permute-start | bytes 430088 | tf_op jit(solution)/shard_map/ppermute | solution.py:217
  98.8 9.8 %collective-permute-start.7 = (bf16[4,14,640]{2,1,0:T(8,128)(2,1)S(1)}, bf16[4,14,640]{2,1,0:T(8,128)(2,1)S(1)}, u32[]{:S(2)}, u32[]{:S(2)}) collective-permute-start(bf16[4,14,640]{2,1,0:T(8,128)(2,1)S(1)} %get-tuple-element.76), channel_id=1, source_target_pairs={{7,0},{6,1},{5,2},{4,3},{11,4},{10,5},{9,6},{8,7},{15,8},{14,9},{1... | collective-permute-start | bytes 215048 | tf_op jit(solution)/shard_map/ppermute | solution.py:217
  99.5 9.8 %collective-permute-start.8 = (bf16[4,14,640]{2,1,0:T(8,128)(2,1)S(1)}, bf16[4,14,640]{2,1,0:T(8,128)(2,1)S(1)}, u32[]{:S(2)}, u32[]{:S(2)}) collective-permute-start(bf16[4,14,640]{2,1,0:T(8,128)(2,1)S(1)} %get-tuple-element.78), channel_id=1, source_target_pairs={{6,0},{7,1},{4,2},{5,3},{10,4},{11,5},{8,6},{9,7},{14,8},{15,9},{1... | collective-permute-start | bytes 215048 | tf_op jit(solution)/shard_map/ppermute | solution.py:217
  100.1 9.8 %collective-permute-start.9 = (bf16[4,14,640]{2,1,0:T(8,128)(2,1)S(1)}, bf16[4,14,640]{2,1,0:T(8,128)(2,1)S(1)}, u32[]{:S(2)}, u32[]{:S(2)}) collective-permute-start(bf16[4,14,640]{2,1,0:T(8,128)(2,1)S(1)} %get-tuple-element.77), channel_id=1, source_target_pairs={{5,0},{4,1},{7,2},{6,3},{9,4},{8,5},{11,6},{10,7},{13,8},{12,9},{1... | collective-permute-start | bytes 215048 | tf_op jit(solution)/shard_map/ppermute | solution.py:217
  100.8 9.8 %collective-permute-start.10 = (bf16[4,14,640]{2,1,0:T(8,128)(2,1)S(1)}, bf16[4,14,640]{2,1,0:T(8,128)(2,1)S(1)}, u32[]{:S(2)}, u32[]{:S(2)}) collective-permute-start(bf16[4,14,640]{2,1,0:T(8,128)(2,1)S(1)} %get-tuple-element.75), channel_id=1, source_target_pairs={{4,0},{5,1},{6,2},{7,3},{8,4},{9,5},{10,6},{11,7},{12,8},{13,9},{1... | collective-permute-start | bytes 215048 | tf_op jit(solution)/shard_map/ppermute | solution.py:217
  121.8 7.8 %collective-permute-start.11 = (bf16[4,14,512]{2,1,0:T(8,128)(2,1)S(1)}, bf16[4,14,512]{2,1,0:T(8,128)(2,1)S(1)}, u32[]{:S(2)}, u32[]{:S(2)}) collective-permute-start(bf16[4,14,512]{2,1,0:T(8,128)(2,1)S(1)} %get-tuple-element.92), channel_id=1, source_target_pairs={{31,0},{30,1},{29,2},{28,3},{3,4},{2,5},{1,6},{0,7},{7,8},{6,9},{5... | collective-permute-start | bytes 172040 | tf_op jit(solution)/shard_map/ppermute | solution.py:217
  122.4 7.9 %collective-permute-start.12 = (bf16[4,14,512]{2,1,0:T(8,128)(2,1)S(1)}, bf16[4,14,512]{2,1,0:T(8,128)(2,1)S(1)}, u32[]{:S(2)}, u32[]{:S(2)}) collective-permute-start(bf16[4,14,512]{2,1,0:T(8,128)(2,1)S(1)} %get-tuple-element.91), channel_id=1, source_target_pairs={{30,0},{31,1},{28,2},{29,3},{2,4},{3,5},{0,6},{1,7},{6,8},{7,9},{4... | collective-permute-start | bytes 172040 | tf_op jit(solution)/shard_map/ppermute | solution.py:217
  124.5 8.6 %collective-permute-start.13 = (bf16[4,14,512]{2,1,0:T(8,128)(2,1)S(1)}, bf16[4,14,512]{2,1,0:T(8,128)(2,1)S(1)}, u32[]{:S(2)}, u32[]{:S(2)}) collective-permute-start(bf16[4,14,512]{2,1,0:T(8,128)(2,1)S(1)} %get-tuple-element.90), channel_id=1, source_target_pairs={{29,0},{28,1},{31,2},{30,3},{1,4},{0,5},{3,6},{2,7},{5,8},{4,9},{7... | collective-permute-start | bytes 172040 | tf_op jit(solution)/shard_map/ppermute | solution.py:217
  125.8 9.8 %collective-permute-start.14 = (bf16[4,14,512]{2,1,0:T(8,128)(2,1)S(1)}, bf16[4,14,512]{2,1,0:T(8,128)(2,1)S(1)}, u32[]{:S(2)}, u32[]{:S(2)}) collective-permute-start(bf16[4,14,512]{2,1,0:T(8,128)(2,1)S(1)} %get-tuple-element.89), channel_id=1, source_target_pairs={{28,0},{29,1},{30,2},{31,3},{0,4},{1,5},{2,6},{3,7},{4,8},{5,9},{6... | collective-permute-start | bytes 172040 | tf_op jit(solution)/shard_map/ppermute | solution.py:217
  126.8 10.2 %collective-permute-start.15 = (bf16[8,14,512]{2,1,0:T(8,128)(2,1)S(1)}, bf16[8,14,512]{2,1,0:T(8,128)(2,1)S(1)}, u32[]{:S(2)}, u32[]{:S(2)}) collective-permute-start(bf16[8,14,512]{2,1,0:T(8,128)(2,1)S(1)} %get-tuple-element.66), channel_id=1, source_target_pairs={{3,0},{2,1},{1,2},{0,3},{7,4},{6,5},{5,6},{4,7},{11,8},{10,9},{9,1... | collective-permute-start | bytes 344072 | tf_op jit(solution)/shard_map/ppermute | solution.py:217
  129.6 10.2 %collective-permute-start.16 = (bf16[8,14,512]{2,1,0:T(8,128)(2,1)S(1)}, bf16[8,14,512]{2,1,0:T(8,128)(2,1)S(1)}, u32[]{:S(2)}, u32[]{:S(2)}) collective-permute-start(bf16[8,14,512]{2,1,0:T(8,128)(2,1)S(1)} %get-tuple-element.65), channel_id=1, source_target_pairs={{2,0},{3,1},{0,2},{1,3},{6,4},{7,5},{4,6},{5,7},{10,8},{11,9},{8,1... | collective-permute-start | bytes 344072 | tf_op jit(solution)/shard_map/ppermute | solution.py:217
  130.3 10.9 %collective-permute-start.17 = (bf16[8,14,512]{2,1,0:T(8,128)(2,1)S(1)}, bf16[8,14,512]{2,1,0:T(8,128)(2,1)S(1)}, u32[]{:S(2)}, u32[]{:S(2)}) collective-permute-start(bf16[8,14,512]{2,1,0:T(8,128)(2,1)S(1)} %get-tuple-element.55), channel_id=1, source_target_pairs={{1,0},{0,1},{3,2},{2,3},{5,4},{4,5},{7,6},{6,7},{9,8},{8,9},{11,10... | collective-permute-start | bytes 344072 | tf_op jit(solution)/shard_map/ppermute | solution.py:217
  133.1 8.7 %collective-permute-start.18 = (bf16[4,14,512]{2,1,0:T(8,128)(2,1)S(1)}, bf16[4,14,512]{2,1,0:T(8,128)(2,1)S(1)}, u32[]{:S(2)}, u32[]{:S(2)}) collective-permute-start(bf16[4,14,512]{2,1,0:T(8,128)(2,1)S(1)} %get-tuple-element.86), channel_id=1, source_target_pairs={{7,0},{6,1},{5,2},{4,3},{11,4},{10,5},{9,6},{8,7},{15,8},{14,9},{1... | collective-permute-start | bytes 172040 | tf_op jit(solution)/shard_map/ppermute | solution.py:217
  135.6 6.9 %collective-permute-start.19 = (bf16[4,14,512]{2,1,0:T(8,128)(2,1)S(1)}, bf16[4,14,512]{2,1,0:T(8,128)(2,1)S(1)}, u32[]{:S(2)}, u32[]{:S(2)}) collective-permute-start(bf16[4,14,512]{2,1,0:T(8,128)(2,1)S(1)} %get-tuple-element.88), channel_id=1, source_target_pairs={{6,0},{7,1},{4,2},{5,3},{10,4},{11,5},{8,6},{9,7},{14,8},{15,9},{1... | collective-permute-start | bytes 172040 | tf_op jit(solution)/shard_map/ppermute | solution.py:217
  136.9 6.2 %collective-permute-start.20 = (bf16[4,14,512]{2,1,0:T(8,128)(2,1)S(1)}, bf16[4,14,512]{2,1,0:T(8,128)(2,1)S(1)}, u32[]{:S(2)}, u32[]{:S(2)}) collective-permute-start(bf16[4,14,512]{2,1,0:T(8,128)(2,1)S(1)} %get-tuple-element.87), channel_id=1, source_target_pairs={{5,0},{4,1},{7,2},{6,3},{9,4},{8,5},{11,6},{10,7},{13,8},{12,9},{1... | collective-permute-start | bytes 172040 | tf_op jit(solution)/shard_map/ppermute | solution.py:217
  139.9 4.3 %collective-permute-start.21 = (bf16[4,14,512]{2,1,0:T(8,128)(2,1)S(1)}, bf16[4,14,512]{2,1,0:T(8,128)(2,1)S(1)}, u32[]{:S(2)}, u32[]{:S(2)}) collective-permute-start(bf16[4,14,512]{2,1,0:T(8,128)(2,1)S(1)} %get-tuple-element.85), channel_id=1, source_target_pairs={{4,0},{5,1},{6,2},{7,3},{8,4},{9,5},{10,6},{11,7},{12,8},{13,9},{1... | collective-permute-start | bytes 172040 | tf_op jit(solution)/shard_map/ppermute | solution.py:217
  146.1 76.8 %copy-start.6 = (f32[8,512]{1,0:T(8,128)S(1)}, f32[8,512]{1,0:T(8,128)}, u32[]{:S(2)}) copy-start(f32[8,512]{1,0:T(8,128)} %get-tuple-element.156) | copy-start | bytes 49156
  146.1 76.8 %copy-start.7 = (f32[8,512]{1,0:T(8,128)S(1)}, f32[8,512]{1,0:T(8,128)}, u32[]{:S(2)}) copy-start(f32[8,512]{1,0:T(8,128)} %get-tuple-element.118) | copy-start | bytes 49156
  146.2 76.8 %copy-start.8 = (f32[8,512]{1,0:T(8,128)S(1)}, f32[8,512]{1,0:T(8,128)}, u32[]{:S(2)}) copy-start(f32[8,512]{1,0:T(8,128)} %get-tuple-element.159) | copy-start | bytes 49156
  146.2 76.8 %copy-start.9 = (s32[8,512]{1,0:T(8,128)S(1)}, s32[8,512]{1,0:T(8,128)}, u32[]{:S(2)}) copy-start(s32[8,512]{1,0:T(8,128)} %add_bitcast_fusion) | copy-start | bytes 49156
  146.2 76.8 %copy-start.22 = (f32[8]{0:T(128)S(1)}, f32[8]{0:T(128)}, u32[]{:S(2)}) copy-start(f32[8]{0:T(128)} %get-tuple-element.143) | copy-start | bytes 100
  146.2 76.8 %copy-start.24 = (f32[8]{0:T(128)S(1)}, f32[8]{0:T(128)}, u32[]{:S(2)}) copy-start(f32[8]{0:T(128)} %get-tuple-element.144) | copy-start | bytes 100
  146.2 76.8 %copy-start.26 = (f32[8]{0:T(128)S(1)}, f32[8]{0:T(128)}, u32[]{:S(2)}) copy-start(f32[8]{0:T(128)} %get-tuple-element.145) | copy-start | bytes 100
  146.2 76.8 %copy-start.28 = (f32[8]{0:T(128)S(1)}, f32[8]{0:T(128)}, u32[]{:S(2)}) copy-start(f32[8]{0:T(128)} %get-tuple-element.168) | copy-start | bytes 100
  146.2 76.8 %copy-start.30 = (f32[8]{0:T(128)S(1)}, f32[8]{0:T(128)}, u32[]{:S(2)}) copy-start(f32[8]{0:T(128)} %get-tuple-element.169) | copy-start | bytes 100
  146.2 76.8 %copy-start.32 = (f32[8]{0:T(128)S(1)}, f32[8]{0:T(128)}, u32[]{:S(2)}) copy-start(f32[8]{0:T(128)} %get-tuple-element.170) | copy-start | bytes 100
  146.2 76.8 %copy-start.34 = (f32[8]{0:T(128)S(1)}, f32[8]{0:T(128)}, u32[]{:S(2)}) copy-start(f32[8]{0:T(128)} %get-tuple-element.171) | copy-start | bytes 100
  146.2 77.6 %copy-start.3 = (f32[8,40,512]{2,1,0:T(8,128)S(1)}, f32[8,40,512]{2,1,0:T(8,128)}, u32[]{:S(2)}) copy-start(f32[8,40,512]{2,1,0:T(8,128)} %get-tuple-element.84) | copy-start | bytes 1966084
  146.5 77.3 %copy-start.14 = (f32[8,512]{1,0:T(8,128)S(1)}, f32[8,512]{1,0:T(8,128)}, u32[]{:S(2)}) copy-start(f32[8,512]{1,0:T(8,128)} %get-tuple-element.125) | copy-start | bytes 49156
  146.6 77.3 %copy-start.15 = (f32[8,512]{1,0:T(8,128)S(1)}, f32[8,512]{1,0:T(8,128)}, u32[]{:S(2)}) copy-start(f32[8,512]{1,0:T(8,128)} %get-tuple-element.158) | copy-start | bytes 49156
  146.6 77.3 %copy-start.16 = (f32[8,512]{1,0:T(8,128)S(1)}, f32[8,512]{1,0:T(8,128)}, u32[]{:S(2)}) copy-start(f32[8,512]{1,0:T(8,128)} %get-tuple-element.116) | copy-start | bytes 49156
  146.6 77.3 %copy-start.17 = (f32[8,512]{1,0:T(8,128)S(1)}, f32[8,512]{1,0:T(8,128)}, u32[]{:S(2)}) copy-start(f32[8,512]{1,0:T(8,128)} %get-tuple-element.161) | copy-start | bytes 49156
  146.6 77.3 %copy-start.18 = (s32[8,512]{1,0:T(8,128)S(1)}, s32[8,512]{1,0:T(8,128)}, u32[]{:S(2)}) copy-start(s32[8,512]{1,0:T(8,128)} %get-tuple-element.128) | copy-start | bytes 49156
  146.6 77.3 %copy-start.19 = (s32[8,512]{1,0:T(8,128)S(1)}, s32[8,512]{1,0:T(8,128)}, u32[]{:S(2)}) copy-start(s32[8,512]{1,0:T(8,128)} %get-tuple-element.129) | copy-start | bytes 49156
  146.6 77.3 %copy-start.20 = (s32[8,512]{1,0:T(8,128)S(1)}, s32[8,512]{1,0:T(8,128)}, u32[]{:S(2)}) copy-start(s32[8,512]{1,0:T(8,128)} %get-tuple-element.130) | copy-start | bytes 49156
  146.6 77.3 %copy-start.21 = (s32[8,512]{1,0:T(8,128)S(1)}, s32[8,512]{1,0:T(8,128)}, u32[]{:S(2)}) copy-start(s32[8,512]{1,0:T(8,128)} %get-tuple-element.131) | copy-start | bytes 49156
  246.5 121.2 %copy-start.47 = (f32[128,2]{0,1:T(2,128)S(1)}, f32[128,2]{0,1:T(2,128)}, u32[]{:S(2)}) copy-start(f32[128,2]{0,1:T(2,128)} %fusion.102) | copy-start | bytes 3076
  (25 other events, 221.0 us)
Sparse Core Ops, SparseCore 0:
  253.6 113.3 all-reduce.7
